TPU v7x, 32 devices: a whole 2x2x4 slice. The times are simulated.
32 devices in a mesh: seq: 16 (over z, y, core), ch: 2 (over x).
Axes of the slice: x: 2, y: 2, z: 4, core: 2. Of those that a mesh axis runs over, the one named last changes fastest.
Arguments:
- tokens: int32 [4096], P('seq'), may hold values from 0 to 3
- feature_table: bfloat16 [512, 3, 4096], P(None, None, 'ch'), may hold values from -6 to 6
- short_filter: float32 [3, 7, 4096], P(None, None, 'ch'), may hold values from -2 to 2
- med_filter: bfloat16 [128, 256], P(None, 'ch'), may hold values from -0.5 to 0.5
- med_bias: float32 [4096], P('ch'), may hold values from 0.5 to 1.5
- out_weight: bfloat16 [4096, 4096], P('seq', 'ch'), may hold values from -0.09375 to 0.09375
Outputs:
- scored: bfloat16 [4096, 4096], P('seq', 'ch')
All inputs are finite; a program needn't handle non-finite values.
Results may differ from a plain program's by a relative error of at most 0.01.
Values may be sent and summed in bfloat16 or wider, within the bound.
A program may use at most 128 MiB of HBM per device.

v0:
```python
import jax
import jax.numpy as jnp
import numpy as np
from jax import lax
from jax.sharding import PartitionSpec as P

base_codes = np.array([65, 67, 71, 84], dtype=np.int32)


def from_behind(value, axis, steps):
    count = lax.axis_size(axis)
    initial, last = (max(0, -steps), min(count, count - steps))
    return lax.ppermute(value, axis, [(source, source + steps) for source in range(initial, last)])


def rims(forward_rows, reverse_rows, rim_width):
    start_row = forward_rows.shape[0] - rim_width
    forward = from_behind(forward_rows[start_row:], "seq", 1)
    second = from_behind(reverse_rows[start_row:], "seq", -1)
    return jnp.stack([forward, second])


def toeplitz(filters):
    tap_count = filters.shape[0]
    row_index = jnp.arange(tap_count, dtype=jnp.int32)[:, None]
    col_index = jnp.arange(2 * tap_count - 1, dtype=jnp.int32)[None, :]
    tap_index = row_index - col_index + tap_count - 1
    inside = (tap_index >= 0) & (tap_index < tap_count)
    picked = jnp.take(filters, jnp.clip(tap_index, 0, tap_count - 1), axis=0)
    toeplitz_table = jnp.where(inside[:, :, None], picked, jnp.zeros((), filters.dtype))
    return jnp.transpose(toeplitz_table, (2, 0, 1))


def per_device(tokens, feature_table, short_filter, med_filter, med_bias, out_weight):
    length = tokens.shape[0]
    width_local = feature_table.shape[2]
    short_taps = short_filter.shape[1]
    tap_count = med_filter.shape[0]
    groups_local = med_filter.shape[1]
    group_width = width_local // groups_local
    strand_bases = jnp.stack([tokens, 3 - jnp.flip(tokens, 0)])
    corner = feature_table[base_codes]
    features = jnp.take(corner, strand_bases, axis=0)
    short_rim = rims(features[0], features[1], short_taps - 1)
    extended = jnp.concatenate([short_rim, features], axis=1).astype(jnp.float32)
    short_out = jnp.zeros((2, length, 3, width_local), jnp.float32)
    for shift_index in range(short_taps):
        begin = short_taps - 1 - shift_index
        short_out = (
            short_out + short_filter[:, shift_index, :] * extended[:, begin : begin + length]
        )
    gated_mix = (short_out[:, :, 0] * short_out[:, :, 2]).astype(jnp.bfloat16)
    medium_rim = rims(gated_mix[0], gated_mix[1], tap_count - 1)
    padded = jnp.concatenate([medium_rim, gated_mix], axis=1)
    kernel = toeplitz(med_filter)
    block_count = length // tap_count
    windows = jnp.stack(
        [
            padded[:, block_index * tap_count : block_index * tap_count + 2 * tap_count - 1]
            for block_index in range(block_count)
        ],
        axis=1,
    )
    windows = windows.reshape(2, block_count, 2 * tap_count - 1, groups_local, group_width)
    medium = jnp.einsum("grw,snwgc->snrgc", kernel, windows, preferred_element_type=jnp.float32)
    medium = medium.reshape(2, length, width_local) + med_bias * gated_mix.astype(jnp.float32)
    hidden = (short_out[:, :, 1] * medium).astype(jnp.bfloat16)
    reverse = hidden[1]
    averaged = (
        0.5 * (hidden[0].astype(jnp.float32) + jnp.flip(reverse, 0).astype(jnp.float32))
    ).astype(jnp.bfloat16)
    gathered = lax.all_gather(averaged, "ch", axis=1, tiled=True)
    weight_rows = lax.all_gather(out_weight, "seq", axis=0, tiled=True)
    result = jnp.dot(gathered, weight_rows, preferred_element_type=jnp.float32)
    return result.astype(jnp.bfloat16)


def solution(mesh):
    placed = (
        P("seq"),
        P(None, None, "ch"),
        P(None, None, "ch"),
        P(None, "ch"),
        P("ch"),
        P("seq", "ch"),
    )
    return jax.shard_map(
        per_device, mesh=mesh, in_specs=placed, out_specs=P("seq", "ch"), check_vma=False
    )
```

profile of v0, /device:TPU:1, one launch (start us, length us, event | category | flops | bytes accessed | tf_op | source)
XLA Modules:
  0.0 461.7 jit_solution(11697910313658378829)
XLA Ops:
  6.5 0.0 copy-start
  6.5 0.7 pad_clamp_fusion.2
  7.2 1.6 gather_fusion
  8.8 0.8 rev.8
  9.6 0.7 compare_select_fusion.2
  10.3 17.1 %gather_fusion.1 = bf16[512,3,2048]{2,1,0:T(4,128)(2,1)} fusion(bf16[4,3,2048]{2,1,0:T(4,128)(2,1)S(1)} %copy.31, s32[1024]{0:T(1024)S(1)} %pad_clamp_fusion.1), kind=kCustom, calls=%fused_computation.1 | custom fusion | bytes 12584960 | tf_op jit(solution)/shard_map/jit(_take)/gather | solution.py:43
  27.3 13.0 %copy.32 = bf16[2,256,3,2048]{1,3,0,2:T(8,128)(2,1)} copy(bf16[2,256,3,2048]{3,2,1,0:T(4,128)(2,1)} %bitcast.65) | data formatting | bytes 12582912 | tf_op jit(solution)/shard_map/jit(_take)/gather | solution.py:43
  40.4 3.3 broadcast_select_fusion
  43.7 2.6 copy-done.2
  46.4 0.9 slice_bitcast_fusion.2
  47.3 0.7 copy.35
  48.0 2.0 collective-permute-start.1
  50.0 0.7 copy.33
  50.7 4.7 %collective-permute-start = (bf16[6,3,2048]{2,0,1:T(8,128)(2,1)S(1)}, bf16[6,3,2048]{2,0,1:T(8,128)(2,1)}, u32[]{:S(2)}, u32[]{:S(2)}) collective-permute-start(bf16[6,3,2048]{2,0,1:T(8,128)(2,1)S(1)} %copy.33), channel_id=1, source_target_pairs={{0,2},{2,4},{4,6},{6,8},{8,10},{10,12},{12,14},{14,16},{16,18},{18... | collective-permute-start | bytes 221192 | tf_op jit(solution)/shard_map/ppermute | solution.py:13
  55.4 0.1 fusion.23
  55.6 0.3 reshape.198
  56.0 65.9 %gather_fusion.2 = bf16[32640,128]{1,0:T(8,128)(2,1)} fusion(bf16[128,128]{1,0:T(8,128)(2,1)S(1)} %copy-done, s32[32768]{0:T(1024)S(1)} %pad_clamp_fusion), kind=kCustom, calls=%fused_computation.2 | custom fusion | bytes 16842240 | tf_op jit(solution)/shard_map/jit(_take)/gather | solution.py:29
  121.9 9.7 %reshape.197 = bf16[128,255,128]{2,1,0:T(8,128)(2,1)} reshape(bf16[32640,128]{1,0:T(8,128)(2,1)} %gather_fusion.2) | data formatting | bytes 16711680 | tf_op jit(solution)/shard_map/jit(_take)/gather | solution.py:29
  131.7 0.1 fusion.21
  131.8 0.0 collective-permute-done.1
  131.8 0.9 copy.36
  132.7 0.0 collective-permute-done
  132.7 1.7 copy.34
  134.4 10.5 %maximum_convert_fusion = f32[2,262,3,2048]{1,3,0,2:T(8,128)} fusion(bf16[2,256,3,2048]{1,3,0,2:T(8,128)(2,1)} %copy-done.2, bf16[1,6,3,2048]{1,3,0,2:T(8,128)(2,1)S(1)} %bitcast.68, bf16[1,6,3,2048]{1,3,0,2:T(8,128)(2,1)S(1)} %bitcast.69), kind=kLoop, calls=%fused_computation.16 | loop fusion | flops 19316736 | bytes 19316736 | tf_op jit(solution)/shard_map/convert_element_type | solution.py:45
  144.8 46.7 %fusion = f32[2,256,3,2048]{1,3,0,2:T(8,128)} fusion(f32[2,262,3,2048]{1,3,0,2:T(8,128)} %maximum_convert_fusion, f32[3,2048]{1,0:T(4,128)S(1)} %get-tuple-element.18, f32[3,2048]{1,0:T(4,128)S(1)} %get-tuple-element.19, f32[3,2048]{1,0:T(4,128)S(1)} %get-tuple-element.20, f32[3,2048]{1,0:T(4,128)S(1)} %get-tuple-element.21, ...), kind=kLoop, calls=%fused_computation.4 | loop fusion | flops 40894464 | bytes 100835328 | tf_op jit(solution)/shard_map/add | solution.py:50
  191.5 3.9 fusion.14
  195.4 1.4 copy-done.4
  196.8 1.3 slice_bitcast_fusion.6
  198.2 1.9 collective-permute-start.3
  200.1 3.9 collective-permute-start.2
  203.9 13.6 %select_bitcast_fusion = bf16[128,128,255,1,1]{0,2,1,4,3:T(8,128)(2,1)} fusion(bf16[128,255,128]{2,1,0:T(8,128)(2,1)} %reshape.197, pred[128,255]{1,0:T(8,128)(4,1)S(1)} %get-tuple-element.24, pred[128,255]{1,0:T(8,128)(4,1)S(1)} %get-tuple-element.25), kind=kLoop, calls=%fused_computation.17 | loop fusion | flops 8355840 | bytes 16776960 | tf_op jit(solution)/shard_map/jit(_where)/select_n | solution.py:30
  217.6 12.7 %copy.41 = bf16[128,128,255,1,1]{2,1,4,3,0:T(8,128)(2,1)} copy(bf16[128,128,255,1,1]{0,2,1,4,3:T(8,128)(2,1)} %select_bitcast_fusion) | data formatting | bytes 16711680 | tf_op jit(solution)/shard_map/jit(_where)/select_n | solution.py:30
  230.3 0.0 collective-permute-done.3
  230.3 0.0 collective-permute-done.2
  230.3 6.0 %pad_maximum_fusion.1 = (bf16[2,255,2048]{1,2,0:T(8,128)(2,1)}, bf16[2,255,2048]{1,2,0:T(8,128)(2,1)}) fusion(bf16[2,256,2048]{1,2,0:T(8,128)(2,1)} %copy-done.4, bf16[1,127,2048]{1,2,0:T(8,128)(2,1)S(1)} %bitcast.70, bf16[1,127,2048]{1,2,0:T(8,128)(2,1)S(1)} %bitcast.71), kind=kLoop, calls=%fused_computation.30 | loop fusion | flops 6266880 | bytes 9412608 | tf_op jit(solution)/shard_map/concatenate | solution.py:54
  236.3 7.2 %fusion.11 = f32[2,2,128,128,16]{2,4,1,0,3:T(8,128)} fusion(bf16[128,128,255,1,1]{2,1,4,3,0:T(8,128)(2,1)S(1)} %copy-done.3, bf16[2,1,255,128,16]{2,4,3,0,1:T(8,128)(2,1)} %bitcast.67, bf16[2,1,255,128,16]{2,4,3,0,1:T(8,128)(2,1)} %bitcast.66), kind=kOutput, calls=%fused_computation.28 | convolution fusion | flops 536862720 | bytes 16728064 | tf_op jit(solution)/shard_map/grw,snwgc->snrgc/dot_general | solution.py:65
  243.5 6.4 %copy.40 = f32[2,2,128,128,16]{2,1,4,3,0:T(2,128)} copy(f32[2,2,128,128,16]{2,4,1,0,3:T(8,128)} %fusion.11) | data formatting | bytes 8388608 | tf_op jit(solution)/shard_map/grw,snwgc->snrgc/transpose | solution.py:65
  249.9 6.4 %reshape.178 = f32[2,256,2048]{1,2,0:T(8,128)} reshape(f32[2,2,128,128,16]{2,1,4,3,0:T(2,128)} %copy.40) | data formatting | bytes 8388608 | tf_op jit(solution)/shard_map/reshape | solution.py:66
  256.3 6.3 %fusion.8 = bf16[2,256,2048]{1,2,0:T(8,128)(2,1)S(1)} fusion(f32[2,256,3,2048]{1,3,0,2:T(8,128)} %fusion, f32[2,256,2048]{1,2,0:T(8,128)} %reshape.178, f32[2048]{0:T(1024)S(1)} %copy-done.7), kind=kLoop, calls=%fused_computation.23 | loop fusion | flops 7340032 | bytes 18882560 | tf_op jit(solution)/shard_map/convert_element_type | solution.py:67
  262.7 1.0 slice_bitcast_fusion.3
  263.7 13.7 %rev.9 = bf16[256,2048]{0,1:T(8,128)(2,1)S(1)} reverse(bf16[256,2048]{0,1:T(8,128)(2,1)} %slice_bitcast_fusion.3), dimensions={0} | reverse | bytes 2097152 | tf_op jit(solution)/shard_map/jit(_flip)/rev | solution.py:70
  277.4 1.3 fusion.16
  278.7 0.0 all-gather.3.cloned.1.call-update
  278.7 0.0 all-gather.5.cloned.1.call-start
  278.8 0.7 all-gather.5.cloned.1.call-update
  279.5 34.0 %all-gather.3.cloned.1.call-done = bf16[256,4096]{0,1:T(8,128)(2,1)} async-done(((bf16[256,2048]{0,1:T(8,128)(2,1)}), bf16[256,4096]{0,1:T(8,128)(2,1)}) %all-gather.3.cloned.1.call-update) | async-done | bytes 2097168 | tf_op jit(solution)/shard_map/all_gather | solution.py:72
  313.5 129.5 %all-gather.5.cloned.1.call-done = bf16[4096,2048]{1,0:T(8,128)(2,1)} async-done(((bf16[256,2048]{1,0:T(8,128)(2,1)}), bf16[4096,2048]{1,0:T(8,128)(2,1)}) %all-gather.5.cloned.1.call-update) | async-done | bytes 16777232 | tf_op jit(solution)/shard_map/all_gather | solution.py:73
  443.0 11.9 %convolution_convert_fusion = bf16[256,2048]{1,0:T(8,128)(2,1)} fusion(bf16[256,4096]{0,1:T(8,128)(2,1)} %all-gather.3.cloned.1.call-done, bf16[4096,2048]{1,0:T(8,128)(2,1)} %all-gather.5.cloned.1.call-done), kind=kOutput, calls=%fused_computation.27 | convolution fusion | flops 4295491584 | bytes 19922944 | tf_op jit(solution)/shard_map/dot_general | solution.py:74
  (24 shorter events, 0.3 us)
Async XLA Ops:
  6.5 49.4 %copy-start = (bf16[128,128]{1,0:T(8,128)(2,1)S(1)}, bf16[128,128]{1,0:T(8,128)(2,1)}, u32[]{:S(2)}) copy-start(bf16[128,128]{1,0:T(8,128)(2,1)} %param.11) | copy-start | bytes 98308
  6.5 307.0 %all-gather.3.cloned.1.call-start = ((), (), s32[]{:S(2)}) async-start(), calls=%async_computation | async-start | bytes 3145728 | tf_op jit(solution)/shard_map/all_gather | solution.py:72
  27.3 13.0 %copy-start.6 = (s32[256]{0:T(256)S(1)}, s32[256]{0:T(256)}, u32[]{:S(2)}) copy-start(s32[256]{0:T(256)} %param.8) | copy-start | bytes 3076
  43.7 2.6 copy-start.2
  46.4 9.1 %copy-start.5 = (f32[3,7,2048]{2,1,0:T(8,128)S(1)}, f32[3,7,2048]{2,1,0:T(8,128)}, u32[]{:S(2)}) copy-start(f32[3,7,2048]{2,1,0:T(8,128)} %param.10) | copy-start | bytes 516100
  48.0 83.8 %collective-permute-start.1 = (bf16[6,3,2048]{2,0,1:T(8,128)(2,1)S(1)}, bf16[6,3,2048]{2,0,1:T(8,128)(2,1)S(1)}, u32[]{:S(2)}, u32[]{:S(2)}) collective-permute-start(bf16[6,3,2048]{2,0,1:T(8,128)(2,1)S(1)} %copy.35), channel_id=1, source_target_pairs={{2,0},{4,2},{6,4},{8,6},{10,8},{12,10},{14,12},{16,14},{18,16},{20... | collective-permute-start | bytes 221192 | tf_op jit(solution)/shard_map/ppermute | solution.py:13
  50.7 82.0 %collective-permute-start = (bf16[6,3,2048]{2,0,1:T(8,128)(2,1)S(1)}, bf16[6,3,2048]{2,0,1:T(8,128)(2,1)}, u32[]{:S(2)}, u32[]{:S(2)}) collective-permute-start(bf16[6,3,2048]{2,0,1:T(8,128)(2,1)S(1)} %copy.33), channel_id=1, source_target_pairs={{0,2},{2,4},{4,6},{6,8},{8,10},{10,12},{12,14},{14,16},{16,18},{18... | collective-permute-start | bytes 221192 | tf_op jit(solution)/shard_map/ppermute | solution.py:13
  195.4 1.4 copy-start.4
  198.2 32.1 %collective-permute-start.3 = (bf16[127,2048]{0,1:T(8,128)(2,1)}, bf16[127,2048]{0,1:T(8,128)(2,1)S(1)}, u32[]{:S(2)}, u32[]{:S(2)}) collective-permute-start(bf16[127,2048]{0,1:T(8,128)(2,1)} %get-tuple-element.10), channel_id=1, source_target_pairs={{2,0},{4,2},{6,4},{8,6},{10,8},{12,10},{14,12},{16,14},{18,16},{20... | collective-permute-start | bytes 1560584 | tf_op jit(solution)/shard_map/ppermute | solution.py:13
  200.1 30.2 %collective-permute-start.2 = (bf16[127,2048]{0,1:T(8,128)(2,1)}, bf16[127,2048]{0,1:T(8,128)(2,1)S(1)}, u32[]{:S(2)}, u32[]{:S(2)}) collective-permute-start(bf16[127,2048]{0,1:T(8,128)(2,1)} %get-tuple-element.9), channel_id=1, source_target_pairs={{0,2},{2,4},{4,6},{6,8},{8,10},{10,12},{12,14},{14,16},{16,18},{18... | collective-permute-start | bytes 1560584 | tf_op jit(solution)/shard_map/ppermute | solution.py:13
  230.3 6.0 %copy-start.3 = (bf16[128,128,255,1,1]{2,1,4,3,0:T(8,128)(2,1)S(1)}, bf16[128,128,255,1,1]{2,1,4,3,0:T(8,128)(2,1)}, u32[]{:S(2)}) copy-start(bf16[128,128,255,1,1]{2,1,4,3,0:T(8,128)(2,1)} %copy.41) | copy-start | bytes 25067524
  249.9 6.4 %copy-start.7 = (f32[2048]{0:T(1024)S(1)}, f32[2048]{0:T(1024)}, u32[]{:S(2)}) copy-start(f32[2048]{0:T(1024)} %param.12) | copy-start | bytes 24580
  278.7 164.3 %all-gather.5.cloned.1.call-start = ((), (), s32[]{:S(2)}) async-start(), calls=%async_computation.1 | async-start | bytes 17825792 | tf_op jit(solution)/shard_map/all_gather | solution.py:73
  443.0 11.9 %copy-start.1 = (bf16[128,128]{1,0:T(8,128)(2,1)S(1)}, bf16[128,128]{1,0:T(8,128)(2,1)}, u32[]{:S(2)}) copy-start(bf16[128,128]{1,0:T(8,128)(2,1)} %param.11) | copy-start | bytes 98308
Sparse Core Ops, SparseCore 0:
  278.9 34.5 all-gather.2
  315.7 127.3 all-gather.4
where the time goes:
time: 465 us; the launch traced here: 462 us
  waiting for transfers between devices  164 us (35%)
  local copies, waits for them, and re-layouts  159 us (34%)
  other arithmetic  93.2 us (20%)
  matrix products  19.1 us (4%)
  between operations  13.6 us (3%)
  starting transfers between devices  12.4 us (3%)
    all_gather x1, waiting for transfers between devices, per_device(): weight_rows = lax.all_gather(out_weight, 'seq', axis=0, tiled=True)  130 us
    gather x2, local copies, waits for them, and re-layouts, toeplitz(): picked = jnp.take(filters, jnp.clip(tap_index, 0, tap_count - 1), axis=0)  75.7 us
    add x1, other arithmetic, per_device(): short_out + short_filter[:, shift_index, :] * extended[:, begin:begin + l...  46.7 us
    all_gather x1, waiting for transfers between devices, per_device(): gathered = lax.all_gather(averaged, 'ch', axis=1, tiled=True)  34 us
    gather x2, local copies, waits for them, and re-layouts, per_device(): features = jnp.take(corner, strand_bases, axis=0)  30.1 us
    rev x1, local copies, waits for them, and re-layouts, per_device(): jnp.flip(reverse, 0).astype(jnp.float32)  13.7 us
    select_n x1, other arithmetic, toeplitz(): jnp.where(inside[:, :, None], picked, jnp.zeros((), filters.dtype))  13.6 us
    select_n x1, local copies, waits for them, and re-layouts, toeplitz(): jnp.where(inside[:, :, None], picked, jnp.zeros((), filters.dtype))  12.7 us
  transfers between devices with their start and end apart: 6, of which 2 were waited for; matrix products, arithmetic and copies ran while one was open for 23% of the time, Pallas kernels for 0%

commit v1 on v0

v1 whole, which is shorter than its diff:
```python
import functools

import jax
import jax.numpy as jnp
from jax import lax
from jax.experimental import pallas as pl
from jax.experimental.pallas import tpu as pltpu
from jax.sharding import PartitionSpec as P

BASE_CODES = (65, 67, 71, 84)
LANES = 128


def hidden_kernel(taps, group_width, hot_f, hot_r, coef, base_f, base_r, bias, out):
    length = out.shape[0]
    blocks = length // taps
    groups = LANES // group_width
    lane_group = lax.broadcasted_iota(jnp.int32, (taps, LANES), 1) // group_width

    def dot(a, b):
        return jnp.dot(a, b, preferred_element_type=jnp.float32)

    def strand(hot, base, first):
        rows = hot[...]
        gate = (dot(rows, coef[0]) * dot(rows, coef[2])).astype(jnp.bfloat16)
        middle = dot(rows[first : first + length], coef[1])
        window = jnp.concatenate(
            [gate[n * taps : (n + 2) * taps] for n in range(blocks)], axis=1
        )
        mixed = [jnp.zeros((taps, LANES), jnp.float32) for _ in range(blocks)]
        for g in range(groups):
            row = jnp.broadcast_to(base[0, g : g + 1, :], (taps, 2 * taps))
            toeplitz = pltpu.roll(row, 0, 1, stride=1, stride_axis=0).astype(jnp.bfloat16)
            product = dot(toeplitz, window)
            for n in range(blocks):
                mixed[n] = jnp.where(
                    lane_group == g, product[:, n * LANES : (n + 1) * LANES], mixed[n]
                )
        own = gate[first : first + length].astype(jnp.float32)
        total = jnp.concatenate(mixed, axis=0) + bias[0] * own
        return (middle * total).astype(jnp.bfloat16).astype(jnp.float32)

    forward = strand(hot_f, base_f, taps)
    reverse = strand(hot_r, base_r, 0)
    out[...] = (0.5 * (forward + reverse)).astype(jnp.bfloat16)


def one_hot(codes, offset, count, step, short_taps):
    picked = jnp.stack(
        [codes[offset + step * k : offset + step * k + count] for k in range(short_taps)], axis=1
    )
    hot = (picked[:, :, None] == jnp.arange(4, dtype=jnp.int32)).astype(jnp.bfloat16)
    hot = hot.reshape(count, 4 * short_taps)
    return jnp.pad(jnp.concatenate([hot, hot], 1), ((0, 0), (0, LANES - 8 * short_taps)))


def coefficients(feature_table, short_filter):
    corner = jnp.stack([feature_table[code] for code in BASE_CODES])
    product = short_filter[:, :, None, :] * jnp.transpose(corner, (1, 0, 2)).astype(jnp.float32)[:, None]
    product = product.reshape(3, -1, product.shape[-1])
    high = lax.reduce_precision(product, 8, 7)
    low = (product - high).astype(jnp.bfloat16)
    both = jnp.concatenate([high.astype(jnp.bfloat16), low], axis=1)
    return jnp.pad(both, ((0, 0), (0, LANES - both.shape[1]), (0, 0)))


def hidden(tokens, base_rows, coef, bias, taps, group_width, short_taps, size):
    length = tokens.shape[0]
    index = lax.axis_index("seq")
    before = lax.ppermute(tokens, "seq", [(i, i + 1) for i in range(size - 1)])
    after = lax.ppermute(tokens, "seq", [(i + 1, i) for i in range(size - 1)])
    before = jnp.where(index == 0, -1, before)
    after = jnp.where(index == size - 1, -1, after)
    codes = jnp.concatenate([before, tokens, after])
    flipped = jnp.where(codes < 0, -1, 3 - codes)
    window = length + taps
    hot_f = one_hot(codes, length - taps, window, -1, short_taps)
    hot_r = one_hot(flipped, length, window, 1, short_taps)
    width = coef.shape[2]
    groups = LANES // group_width
    steps = width // LANES
    whole = pl.BlockSpec((window, LANES), lambda i: (0, 0))
    rows = pl.BlockSpec((1, groups, 2 * taps), lambda i: (i, 0, 0))
    return pl.pallas_call(
        functools.partial(hidden_kernel, taps, group_width),
        out_shape=jax.ShapeDtypeStruct((length, width), jnp.bfloat16),
        grid=(steps,),
        in_specs=[
            whole,
            whole,
            pl.BlockSpec((3, LANES, LANES), lambda i: (0, 0, i)),
            rows,
            rows,
            pl.BlockSpec((1, 1, LANES), lambda i: (i, 0, 0)),
        ],
        out_specs=pl.BlockSpec((length, LANES), lambda i: (0, i)),
        compiler_params=pltpu.CompilerParams(vmem_limit_bytes=32 * 1024 * 1024),
        cost_estimate=pl.CostEstimate(
            flops=2 * 2 * length * width * 2 * taps * groups, bytes_accessed=8 * 1024 * 1024, transcendentals=0
        ),
    )(hot_f, hot_r, coef, base_rows[0], base_rows[1], bias.reshape(steps, 1, LANES))


def tap_rows(med_filter, group_width):
    taps = med_filter.shape[0]
    filters = jnp.transpose(med_filter).astype(jnp.float32)
    groups = LANES // group_width
    zeros = jnp.zeros_like(filters)
    reverse = jnp.concatenate([filters, zeros], axis=1)
    flipped = filters[:, ::-1]
    forward = jnp.concatenate([zeros[:, :1], flipped, zeros[:, 1:]], axis=1)
    return [x.reshape(-1, groups, 2 * taps) for x in (forward, reverse)]


def per_device(size, tokens, feature_table, short_filter, med_filter, med_bias, out_weight):
    taps, groups_local = med_filter.shape
    group_width = feature_table.shape[2] // groups_local
    short_taps = short_filter.shape[1]
    weight = lax.all_gather(out_weight, "seq", axis=0, tiled=True)
    coef = coefficients(feature_table, short_filter)
    coef = lax.all_gather(coef, "ch", axis=2, tiled=True)
    med_all = lax.all_gather(med_filter, "ch", axis=1, tiled=True)
    bias = lax.all_gather(med_bias, "ch", axis=0, tiled=True)
    base_rows = tap_rows(med_all, group_width)
    mixed = hidden(tokens, base_rows, coef, bias, taps, group_width, short_taps, size)
    return jnp.dot(mixed, weight, preferred_element_type=jnp.float32).astype(jnp.bfloat16)


def solution(mesh):
    placed = (
        P("seq"),
        P(None, None, "ch"),
        P(None, None, "ch"),
        P(None, "ch"),
        P("ch"),
        P("seq", "ch"),
    )
    return jax.shard_map(
        functools.partial(per_device, mesh.shape["seq"]),
        mesh=mesh,
        in_specs=placed,
        out_specs=P("seq", "ch"),
        check_vma=False,
    )
```

time: 465 us -> 204 us (0.44)
  local copies, waits for them, and re-layouts: 159 us -> 4.42 us
  other arithmetic: 93.2 us -> 3.08 us
  waiting for transfers between devices: 164 us -> 132 us
  Pallas kernels: 0 us -> 28.2 us
  matrix products: 19.1 us -> 9.25 us
  blocking collectives: 0 us -> 7.04 us
  starting transfers between devices: 12.4 us -> 6.5 us
    gather x6 -> x0, local copies, waits for them, and re-layouts: 107 us -> none  [the longest x2 75.7 us: toeplitz(): picked = jnp.take(filters, jnp.clip(tap_index, 0, tap_count - 1), axis=0)]
    add x1 -> x0, other arithmetic: 46.7 us -> none  [per_device(): short_out + short_filter[:, shift_index, :] * extended[:, begin:begin + l...]
    all_gather x2, waiting for transfers between devices: 164 us -> 131 us  [the longest x1 99.4 us: per_device(): weight = lax.all_gather(out_weight, 'seq', axis=0, tiled=True)]
    pallas_call x0 -> x1, Pallas kernels: none -> 28.2 us  [hidden(): pl.pallas_call(functools.partial(hidden_kernel, taps, group_width), out_s...]
    convert_element_type x4 -> x3, other arithmetic: 22 us -> 0.25 us  [the longest x1 0.12 us: coefficients(): both = jnp.concatenate([high.astype(jnp.bfloat16), low], axis=1)]
    select_n x4 -> x3, other arithmetic: 17.7 us -> 0.03 us  [the longest x1 0.01 us: hidden(): flipped = jnp.where(codes < 0, -1, 3 - codes)]
    rev x2 -> x1, local copies, waits for them, and re-layouts: 14.5 us -> 0.08 us  [tap_rows(): flipped = filters[:, ::-1]]
    select_n x2 -> x0, local copies, waits for them, and re-layouts: 13 us -> none  [the longest x1 12.7 us: toeplitz(): jnp.where(inside[:, :, None], picked, jnp.zeros((), filters.dtype))]
  transfers between devices with their start and end apart: 6 -> 4, of which waited for: 2 -> 2; matrix products, arithmetic and copies ran while one was open for 23% -> 1% of each run, Pallas kernels for 0% -> 14%
where the time goes in v1:
time: 204 us
  waiting for transfers between devices  132 us (65%)
  Pallas kernels  28.2 us (14%)
  between operations  13.7 us (7%)
  matrix products  9.25 us (5%)
  blocking collectives  7.04 us (3%)
  starting transfers between devices  6.5 us (3%)
  local copies, waits for them, and re-layouts  4.42 us (2%)
  other arithmetic  3.08 us (2%)
    all_gather x1, waiting for transfers between devices, per_device(): weight = lax.all_gather(out_weight, 'seq', axis=0, tiled=True)  99.4 us
    all_gather x1, waiting for transfers between devices, per_device(): coef = lax.all_gather(coef, 'ch', axis=2, tiled=True)  31.4 us
    pallas_call x1, Pallas kernels, hidden(): pl.pallas_call(functools.partial(hidden_kernel, taps, group_width), out_s...  28.2 us
    dot_general x1, matrix products, per_device(): jnp.dot(mixed, weight, preferred_element_type=jnp.float32)  9.25 us
    ppermute x1, starting transfers between devices, hidden(): before = lax.ppermute(tokens, 'seq', [(i, i + 1) for i in range(size - 1)])  4.54 us
  transfers between devices with their start and end apart: 4, of which 2 were waited for; matrix products, arithmetic and copies ran while one was open for 1% of the time, Pallas kernels for 14%

profile of v1, /device:TPU:1, one launch (start us, length us, event | category | flops | bytes accessed | tf_op | source)
XLA Modules:
  0.0 203.8 jit_solution(8509714662629883262)
XLA Ops:
  6.5 0.0 all-gather.3.cloned.1.call-start
  6.5 1.1 fusion.4
  7.7 0.1 convert_bitcast_fusion.1
  7.8 1.1 broadcast_multiply_fusion
  8.9 0.2 mul.20
  9.2 0.0 copy-start.3
  9.2 0.0 copy-start.1
  9.2 0.1 reduce-precision_convert_fusion
  9.3 0.0 copy-start.2
  9.3 1.4 fusion.2
  10.7 0.0 all-gather.3.cloned.1.call-update
  10.7 0.0 all-gather.5.cloned.1.call-start
  10.8 0.7 all-gather.5.cloned.1.call-update
  11.5 0.0 copy-done.3
  11.5 4.5 %collective-permute-start = (s32[256]{0:T(256)S(1)}, s32[256]{0:T(256)S(1)}, u32[]{:S(2)}, u32[]{:S(2)}) collective-permute-start(s32[256]{0:T(256)S(1)} %copy-done.3), channel_id=1, source_target_pairs={{0,2},{2,4},{4,6},{6,8},{8,10},{10,12},{12,14},{14,16},{16,18},{18... | collective-permute-start | bytes 3080 | tf_op jit(solution)/shard_map/ppermute | solution.py:70
  16.0 1.9 collective-permute-start.1
  18.0 0.0 copy-done.1
  18.0 3.5 %all_gather.13 = bf16[128,256]{1,0:T(8,128)(2,1)S(1)} all-gather(bf16[128,128]{1,0:T(8,128)(2,1)S(1)} %copy-done.1), channel_id=1, replica_groups=mesh['seq'=16,'ch'=2] {'ch'}, dimensions={1}, use_global_device_ids=true | all-gather | bytes 98304 | tf_op jit(solution)/shard_map/all_gather | solution.py:122
  21.5 0.1 rev.3
  21.6 0.1 copy.17
  21.7 0.1 pad.23.clone
  21.8 0.1 maximum_maximum_fusion
  21.9 0.0 copy-done.2
  21.9 3.6 %all_gather.14 = f32[4096]{0:T(1024)S(1)} all-gather(f32[2048]{0:T(1024)S(1)} %copy-done.2), channel_id=1, replica_groups=mesh['seq'=16,'ch'=2] {'ch'}, dimensions={0}, use_global_device_ids=true | all-gather | bytes 24576 | tf_op jit(solution)/shard_map/all_gather | solution.py:123
  25.5 0.1 eq.50
  25.6 0.1 copy.15
  25.7 0.0 collective-permute-done
  25.7 0.0 collective-permute-done.1
  25.8 0.1 fusion.5
  26.0 0.1 fusion.6
  26.2 0.1 broadcast_compare_fusion
  26.3 0.2 copy.14
  26.5 0.2 copy.13
  26.7 31.4 %all-gather.3.cloned.1.call-done.coef = bf16[3,128,4096]{2,1,0:T(8,128)(2,1)} async-done(((bf16[3,128,2048]{2,1,0:T(8,128)(2,1)}), bf16[3,128,4096]{2,1,0:T(8,128)(2,1)}) %all-gather.3.cloned.1.call-update) | async-done | bytes 3145744 | tf_op jit(solution)/shard_map/all_gather | solution.py:121
  58.2 0.0 copy-start
  58.2 1.9 copy-done
  60.1 28.2 %shard_map.64 = bf16[256,4096]{1,0:T(8,128)(2,1)S(1)} custom-call(bf16[384,128]{1,0:T(8,128)(2,1)S(1)} %pad_convert_fusion.1.hot_f, bf16[384,128]{1,0:T(8,128)(2,1)S(1)} %pad_convert_fusion.hot_r, bf16[3,128,4096]{2,1,0:T(8,128)(2,1)S(1)} %copy-done, f32[32,8,256]{2,1,0:T(8,128)S(1)} %bitcast.15, f32[32,8,256]{2,1,0:T(8,128)S(1)} %pad_bitcast_fusion.base_r, ...), custom_call_target="tpu_custom_call" | custom-call | flops 8589934592 | bytes 8388608 | tf_op jit(solution)/shard_map/pallas_call | solution.py:84
  88.2 99.4 %all-gather.5.cloned.1.call-done = bf16[4096,2048]{1,0:T(8,128)(2,1)} async-done(((bf16[256,2048]{1,0:T(8,128)(2,1)}), bf16[4096,2048]{1,0:T(8,128)(2,1)}) %all-gather.5.cloned.1.call-update) | async-done | bytes 16777232 | tf_op jit(solution)/shard_map/all_gather | solution.py:119
  187.7 9.2 %convolution_convert_fusion = bf16[256,2048]{1,0:T(8,128)(2,1)} fusion(bf16[256,4096]{1,0:T(8,128)(2,1)S(1)} %shard_map.64, bf16[4096,2048]{1,0:T(8,128)(2,1)} %all-gather.5.cloned.1.call-done), kind=kOutput, calls=%fused_computation.3 | convolution fusion | flops 4295491584 | bytes 19922944 | tf_op jit(solution)/shard_map/dot_general | solution.py:126
  (32 shorter events, 0.3 us)
Async XLA Ops:
  6.5 51.6 %all-gather.3.cloned.1.call-start = ((), (), s32[]{:S(2)}) async-start(), calls=%async_computation | async-start | bytes 4718592 | tf_op jit(solution)/shard_map/all_gather | solution.py:121
  9.2 2.3 %copy-start.3 = (s32[256]{0:T(256)S(1)}, s32[256]{0:T(256)}, u32[]{:S(2)}) copy-start(s32[256]{0:T(256)} %param.6) | copy-start | bytes 3076
  9.2 8.8 %copy-start.1 = (bf16[128,128]{1,0:T(8,128)(2,1)S(1)}, bf16[128,128]{1,0:T(8,128)(2,1)}, u32[]{:S(2)}) copy-start(bf16[128,128]{1,0:T(8,128)(2,1)} %param.9) | copy-start | bytes 98308
  9.3 12.6 %copy-start.2 = (f32[2048]{0:T(1024)S(1)}, f32[2048]{0:T(1024)}, u32[]{:S(2)}) copy-start(f32[2048]{0:T(1024)} %param.10) | copy-start | bytes 24580
  10.7 176.9 %all-gather.5.cloned.1.call-start = ((), (), s32[]{:S(2)}) async-start(), calls=%async_computation.1 | async-start | bytes 17825792 | tf_op jit(solution)/shard_map/all_gather | solution.py:119
  11.5 14.2 %collective-permute-start = (s32[256]{0:T(256)S(1)}, s32[256]{0:T(256)S(1)}, u32[]{:S(2)}, u32[]{:S(2)}) collective-permute-start(s32[256]{0:T(256)S(1)} %copy-done.3), channel_id=1, source_target_pairs={{0,2},{2,4},{4,6},{6,8},{8,10},{10,12},{12,14},{14,16},{16,18},{18... | collective-permute-start | bytes 3080 | tf_op jit(solution)/shard_map/ppermute | solution.py:70
  16.0 9.7 %collective-permute-start.1 = (s32[256]{0:T(256)S(1)}, s32[256]{0:T(256)S(1)}, u32[]{:S(2)}, u32[]{:S(2)}) collective-permute-start(s32[256]{0:T(256)S(1)} %copy-done.3), channel_id=1, source_target_pairs={{2,0},{4,2},{6,4},{8,6},{10,8},{12,10},{14,12},{16,14},{18,16},{20... | collective-permute-start | bytes 3080 | tf_op jit(solution)/shard_map/ppermute | solution.py:71
  58.2 1.9 copy-start
Sparse Core Ops, SparseCore 0:
  10.9 47.2 all-gather.2
  60.3 127.2 all-gather.4

commit v2 on v0

v2 whole, which is shorter than its diff:
```python
import functools

import jax
import jax.numpy as jnp
from jax import lax
from jax.experimental import pallas as pl
from jax.experimental.pallas import tpu as pltpu
from jax.sharding import PartitionSpec as P

BASE_CODES = (65, 67, 71, 84)
LANES = 128
MESH = pl.DeviceIdType.MESH


def dot(a, b):
    return jnp.dot(a, b, preferred_element_type=jnp.float32)


def hidden_block(taps, group_width, length, hots, tab, base, columns, group_rows):
    count = hots.shape[1] // (length + taps)
    per_block = length // taps
    groups = LANES // group_width
    lane_group = lax.broadcasted_iota(jnp.int32, (taps, LANES), 1) // group_width
    upper = lax.broadcasted_iota(jnp.int32, (8, LANES), 0) < 4
    short_taps = hots.shape[2] // 8 - 1
    coef = []
    for branch in range(3):
        scale = tab[branch, :, columns]
        feature = tab[3 + branch, :, columns]
        parts = []
        for k in range(short_taps):
            product = scale[k : k + 1] * feature
            high = product.astype(jnp.bfloat16).astype(jnp.float32)
            parts.append(jnp.where(upper, high, product - high))
        parts.append(jnp.zeros((8, LANES), jnp.float32))
        coef.append(jnp.concatenate(parts, axis=0).astype(jnp.bfloat16))
    bias = tab[0, :, columns][7:8]
    pair = jnp.concatenate([coef[0], coef[2]], axis=1)
    window_rows = length + taps
    strands = []
    for strand in range(2):
        first = taps if strand == 0 else 0
        rows = hots[strand]
        both = dot(rows, pair)
        gate = (both[:, :LANES] * both[:, LANES:]).astype(jnp.bfloat16)
        starts = [b * window_rows for b in range(count)]
        middle = dot(
            jnp.concatenate([rows[s + first : s + first + length] for s in starts], axis=0), coef[1]
        )
        window = jnp.concatenate(
            [gate[s + n * taps : s + (n + 2) * taps] for s in starts for n in range(per_block)], axis=1
        )
        mixed = [jnp.zeros((taps, LANES), jnp.float32) for _ in range(count * per_block)]
        taps_here = base[strand, group_rows, :]
        for g in range(groups):
            row = jnp.broadcast_to(taps_here[g : g + 1, :], (taps, 2 * taps))
            toeplitz = pltpu.roll(row, 0, 1, stride=1, stride_axis=0).astype(jnp.bfloat16)
            product = dot(toeplitz, window)
            for n in range(count * per_block):
                mixed[n] = jnp.where(
                    lane_group == g, product[:, n * LANES : (n + 1) * LANES], mixed[n]
                )
        own = jnp.concatenate([gate[s + first : s + first + length] for s in starts], axis=0)
        total = jnp.concatenate(mixed, axis=0) + bias * own.astype(jnp.float32)
        strands.append((middle * total).astype(jnp.bfloat16).astype(jnp.float32))
    return (0.5 * (strands[0] + strands[1])).astype(jnp.bfloat16)


def kernel(
    sizes, taps, group_width,
    hots, tab_in, base_in, weight, out,
    tabs, bases, pieces, mixed, stage,
    tab_send, tab_recv, local_sem, y_send, up_send, down_send, side_send, recv, out_send, out_recv,
):
    seq_size, ch_size = sizes
    outer_size = seq_size // 4
    me, ch = lax.axis_index("seq"), lax.axis_index("ch")
    core = lax.rem(me, 2)
    y = lax.rem(me // 2, 2)
    outer = me // 4
    rows, width = weight.shape
    half = width // 2
    length = out.shape[0]
    tile = min(256, half)
    tiles = half // tile

    def place(o, yy, cc):
        return (o * 2 + yy) * 2 + cc

    side, across = place(outer, y, 1 - core), place(outer, 1 - y, core)

    barrier = pltpu.get_barrier_semaphore()
    for other in (side, across):
        pl.semaphore_signal(barrier, inc=1, device_id={"seq": other}, device_id_type=MESH)
    for step in range(1, ch_size):
        pl.semaphore_signal(
            barrier, inc=1, device_id={"ch": lax.rem(ch + step, ch_size)}, device_id_type=MESH
        )

    @pl.when(outer > 0)
    def _():
        pl.semaphore_signal(barrier, inc=1, device_id={"seq": me - 4}, device_id_type=MESH)

    @pl.when(outer < outer_size - 1)
    def _():
        pl.semaphore_signal(barrier, inc=1, device_id={"seq": me + 4}, device_id_type=MESH)

    ends = (outer > 0).astype(jnp.int32) + (outer < outer_size - 1).astype(jnp.int32)
    pl.semaphore_wait(barrier, ch_size + 1 + ends)

    def remote(src, dst, send, receive, other):
        return pltpu.make_async_remote_copy(
            src_ref=src, dst_ref=dst, send_sem=send, recv_sem=receive,
            device_id=other, device_id_type=MESH,
        )

    def piece(o, yy, cc):
        start = pl.multiple_of((yy * 2 + cc) * rows, rows)
        return pieces.at[o, pl.ds(start, rows)]

    def columns_of(which):
        return weight.at[:, pl.ds(pl.multiple_of(which * half, half), half)]

    def sub_y(sub):
        return y if sub == 0 else 1 - y

    def forwards(origin, sub, action, own=False):
        yy = sub_y(sub)
        dst = piece(origin, yy, core)
        src = columns_of(y) if own else dst
        receive = recv.at[origin, yy * 2 + core]

        @pl.when((origin <= outer) & (outer < outer_size - 1))
        def _():
            action(remote(src, dst, up_send.at[origin, sub], receive, {"seq": me + 4}))

        @pl.when((origin >= outer) & (outer > 0))
        def _():
            action(remote(src, dst, down_send.at[origin, sub], receive, {"seq": me - 4}))

        action(remote(src, dst, side_send.at[origin, sub], receive, {"seq": side}))

    def arrived(origin, slot):
        start = pl.multiple_of(slot * rows, rows)
        dst = pieces.at[origin, pl.ds(start, rows)]
        remote(dst, dst, y_send, recv.at[origin, slot], {"seq": across}).wait_recv()

    y_copy = remote(
        columns_of(1 - y), piece(outer, y, core), y_send, recv.at[outer, y * 2 + core], {"seq": across}
    )
    y_copy.start()
    forwards(outer, 0, lambda c: c.start(), own=True)
    tab_copies = []
    for step in range(1, ch_size):
        other = {"ch": lax.rem(ch + step, ch_size)}
        for number, (src, dst) in enumerate(((tab_in, tabs), (base_in, bases))):
            copy = remote(src, dst.at[ch], tab_send.at[number, step], tab_recv.at[number, ch], other)
            copy.start()
            tab_copies.append(copy)
    local_copies = [
        pltpu.make_async_copy(columns_of(y), piece(outer, y, core), local_sem.at[0]),
        pltpu.make_async_copy(tab_in, tabs.at[ch], local_sem.at[1]),
        pltpu.make_async_copy(base_in, bases.at[ch], local_sem.at[2]),
    ]
    for copy in local_copies:
        copy.start()
    for copy in local_copies:
        copy.wait()

    groups = LANES // group_width
    per_ch = width // LANES
    steps = ch_size * per_ch

    def block(i, carry):
        owner = lax.rem(ch + i // per_ch, ch_size)
        inner = lax.rem(i, per_ch)

        @pl.when((inner == 0) & (i > 0))
        def _():
            for number, dst in enumerate((tabs, bases)):
                remote(
                    dst.at[owner], dst.at[owner], tab_send.at[number, 0],
                    tab_recv.at[number, owner], {"ch": lax.rem(ch + 1, ch_size)},
                ).wait_recv()

        value = hidden_block(
            taps, group_width, length, hots, tabs.at[owner], bases.at[owner],
            pl.ds(pl.multiple_of(inner * LANES, LANES), LANES),
            pl.ds(pl.multiple_of(inner * groups, groups), groups),
        )
        mixed[:, pl.ds(pl.multiple_of((owner * per_ch + inner) * LANES, LANES), LANES)] = value
        return carry

    def event(t, sub):
        yy = sub_y(sub)
        if t == 0:
            arrived(outer, yy * 2 + core)
            forwards(outer, sub, lambda c: c.start())
            return

        @pl.when(outer >= t)
        def _():
            arrived(outer - t, yy * 2 + core)
            forwards(outer - t, sub, lambda c: c.start())

        @pl.when(outer + t < outer_size)
        def _():
            arrived(outer + t, yy * 2 + core)
            forwards(outer + t, sub, lambda c: c.start())

    events = [(t, sub) for t in range(outer_size) for sub in range(2)][1:]
    done = 0
    for number, (t, sub) in enumerate(events):
        upto = steps * (number + 1) // len(events)
        if upto > done:
            lax.fori_loop(done, upto, block, 0)
        done = upto
        event(t, sub)

    def side_wait(o, carry):
        for yy in range(2):
            arrived(o, yy * 2 + 1 - core)
        return carry

    lax.fori_loop(0, outer_size, side_wait, 0)

    depth = 4 * rows

    def product(position, n):
        total = None
        for o in range(outer_size):
            part = dot(
                mixed[position : position + length, o * depth : (o + 1) * depth],
                pieces[o, :, n * tile : (n + 1) * tile],
            )
            total = part if total is None else total + part
        return total.astype(jnp.bfloat16)

    def out_columns(n):
        return out.at[:, pl.ds(pl.multiple_of(y * half + n * tile, tile), tile)]

    out_copies = []
    for n in range(tiles):
        stage[n] = product(length, n)
        copy = remote(stage.at[n], out_columns(n), out_send.at[n], out_recv.at[n], {"seq": across})
        copy.start()
        out_copies.append(copy)
    for n in range(tiles):
        out[:, pl.ds(pl.multiple_of(y * half + n * tile, tile), tile)] = product(0, n)

    y_copy.wait_send()
    for copy in tab_copies:
        copy.wait_send()
    for t in range(outer_size):
        for sub in range(2):
            if t == 0:
                forwards(outer, sub, lambda c: c.wait_send(), own=sub == 0)
                continue

            @pl.when(outer >= t)
            def _():
                forwards(outer - t, sub, lambda c: c.wait_send())

            @pl.when(outer + t < outer_size)
            def _():
                forwards(outer + t, sub, lambda c: c.wait_send())

    for n in range(tiles):
        theirs = out.at[:, pl.ds(pl.multiple_of((1 - y) * half + n * tile, tile), tile)]
        out_copies[n].wait_send()
        remote(stage.at[n], theirs, out_send.at[n], out_recv.at[n], {"seq": across}).wait_recv()


def one_hot(codes, offset, count, step, short_taps):
    picked = jnp.stack(
        [lax.dynamic_slice_in_dim(codes, offset + step * k, count) for k in range(short_taps)], axis=1
    )
    hot = picked[:, :, None] == jnp.arange(8, dtype=jnp.int32) % 4
    hot = jnp.pad(hot, ((0, 0), (0, 1), (0, 0)))
    return hot.reshape(count, 8 * (short_taps + 1)).astype(jnp.bfloat16)


def tap_rows(med_filter):
    filters = jnp.transpose(med_filter).astype(jnp.float32)
    zeros = jnp.zeros_like(filters)
    reverse = jnp.concatenate([filters, zeros], axis=1)
    forward = jnp.concatenate([zeros[:, :1], filters[:, ::-1], zeros[:, 1:]], axis=1)
    return jnp.stack([forward, reverse])


def tables(feature_table, short_filter, med_bias):
    corner = jnp.stack([feature_table[code] for code in BASE_CODES] * 2, axis=1).astype(jnp.float32)
    last = jnp.broadcast_to(med_bias, (3, 1, med_bias.shape[0]))
    return jnp.concatenate([jnp.concatenate([short_filter, last], axis=1), corner], axis=0)


def per_device(sizes, tokens, feature_table, short_filter, med_filter, med_bias, out_weight):
    seq_size, ch_size = sizes
    taps, groups_local = med_filter.shape
    rows, width = out_weight.shape
    group_width = width // groups_local
    short_taps = short_filter.shape[1]
    length = tokens.shape[0]
    window = length + taps
    me = lax.axis_index("seq")
    codes = lax.all_gather(tokens, "seq", axis=0, tiled=True)
    flipped = jnp.pad(3 - codes, (length, length), constant_values=-1)
    codes = jnp.pad(codes, (length, length), constant_values=-1)
    hots = [[], []]
    for index in (me, me ^ 2):
        start = (index + 1) * length
        hots[0].append(one_hot(codes, start - taps, window, -1, short_taps))
        hots[1].append(one_hot(flipped, start, window, 1, short_taps))
    hots = jnp.stack([jnp.concatenate(h, axis=0) for h in hots])
    tab = tables(feature_table, short_filter, med_bias)
    base = tap_rows(med_filter)
    outer_size = seq_size // 4
    half = width // 2
    tile = min(256, half)
    tiles = half // tile
    dma = pltpu.SemaphoreType.DMA
    return pl.pallas_call(
        functools.partial(kernel, sizes, taps, group_width),
        out_shape=jax.ShapeDtypeStruct((length, width), jnp.bfloat16),
        in_specs=[pl.BlockSpec(memory_space=pltpu.VMEM)] * 4,
        out_specs=pl.BlockSpec(memory_space=pltpu.VMEM),
        scratch_shapes=[
            pltpu.VMEM((ch_size,) + tab.shape, jnp.float32),
            pltpu.VMEM((ch_size,) + base.shape, jnp.float32),
            pltpu.VMEM((outer_size, 4 * rows, half), jnp.bfloat16),
            pltpu.VMEM((2 * length, ch_size * width), jnp.bfloat16),
            pltpu.VMEM((tiles, length, tile), jnp.bfloat16),
            dma((2, ch_size)),
            dma((2, ch_size)),
            dma((3,)),
            dma,
            dma((outer_size, 2)),
            dma((outer_size, 2)),
            dma((outer_size, 2)),
            dma((outer_size, 4)),
            dma((tiles,)),
            dma((tiles,)),
        ],
        compiler_params=pltpu.CompilerParams(
            collective_id=0, has_side_effects=True, vmem_limit_bytes=50 * 1024 * 1024
        ),
    )(hots, tab, base, out_weight)


def solution(mesh):
    placed = (
        P("seq"),
        P(None, None, "ch"),
        P(None, None, "ch"),
        P(None, "ch"),
        P("ch"),
        P("seq", "ch"),
    )
    sizes = (mesh.shape["seq"], mesh.shape["ch"])
    return jax.shard_map(
        functools.partial(per_device, sizes),
        mesh=mesh,
        in_specs=placed,
        out_specs=P("seq", "ch"),
        check_vma=False,
    )
```

time: 465 us -> 119 us (0.26)
  waiting for transfers between devices: 164 us -> 0 us
  local copies, waits for them, and re-layouts: 159 us -> 6.77 us
  other arithmetic: 93.2 us -> 1.47 us
  Pallas kernels: 0 us -> 87.1 us
  blocking collectives: 0 us -> 23.2 us
  matrix products: 19.1 us -> 0 us
  between operations: 13.6 us -> 0.3 us
  starting transfers between devices: 12.4 us -> 0 us
    all_gather x2 -> x0, waiting for transfers between devices: 164 us -> none  [the longest x1 130 us: per_device(): weight_rows = lax.all_gather(out_weight, 'seq', axis=0, tiled=True)]
    gather x6 -> x0, local copies, waits for them, and re-layouts: 107 us -> none  [the longest x2 75.7 us: toeplitz(): picked = jnp.take(filters, jnp.clip(tap_index, 0, tap_count - 1), axis=0)]
    pallas_call x0 -> x1, Pallas kernels: none -> 87.1 us  [per_device(): pl.pallas_call(functools.partial(kernel, sizes, taps, group_width), out_s...]
    add x1 -> x0, other arithmetic: 46.7 us -> none  [per_device(): short_out + short_filter[:, shift_index, :] * extended[:, begin:begin + l...]
    all_gather x0 -> x1, blocking collectives: none -> 23.2 us  [per_device(): codes = lax.all_gather(tokens, 'seq', axis=0, tiled=True)]
    convert_element_type x4 -> x2, other arithmetic: 22 us -> 0.02 us  [the longest x1 0.02 us: tables(): jnp.stack([feature_table[code] for code in BASE_CODES] * 2, axis=1)]
    dot_general x2 -> x0, matrix products: 19.1 us -> none  [the longest x1 11.9 us: per_device(): result = jnp.dot(gathered, weight_rows, preferred_element_type=jnp.float32)]
    select_n x4 -> x1, other arithmetic: 17.7 us -> 0.01 us  [one_hot(): hot = picked[:, :, None] == jnp.arange(8, dtype=jnp.int32) % 4]
  transfers between devices with their start and end apart: 6 -> 0, of which waited for: 2 -> 0; matrix products, arithmetic and copies ran while one was open for 23% -> 0% of each run, Pallas kernels for 0% -> 0%
where the time goes in v2:
time: 119 us
  Pallas kernels  87.1 us (73%)
  blocking collectives  23.2 us (19%)
  local copies, waits for them, and re-layouts  6.77 us (6%)
  other arithmetic  1.47 us (1%)
    pallas_call x1, Pallas kernels, per_device(): pl.pallas_call(functools.partial(kernel, sizes, taps, group_width), out_s...  87.1 us
    all_gather x1, blocking collectives, per_device(): codes = lax.all_gather(tokens, 'seq', axis=0, tiled=True)  23.2 us
    unnamed x4, local copies, waits for them, and re-layouts  3.06 us

profile of v2, /device:TPU:1, one launch (start us, length us, event | category | flops | bytes accessed | tf_op | source)
XLA Modules:
  0.0 118.8 jit_solution(18230610994230316573)
XLA Ops:
  0.0 0.1 pad.31.clone
  0.1 23.2 %all-gather = s32[16,1,256]{2,1,0:T(1,128)S(1)} all-gather(s32[1,1,256]{2,1,0:T(1,128)} %bitcast.32), channel_id=1, replica_groups=mesh['seq'=16,'ch'=2] {'seq'}, dimensions={0}, use_global_device_ids=true | all-gather | bytes 17408 | tf_op jit(solution)/shard_map/all_gather | solution.py:306
  23.3 0.1 pad_dynamic-slice_fusion.27
  23.4 0.2 pad_dynamic-slice_fusion.21
  23.7 0.1 pad_dynamic-slice_fusion.13
  23.8 0.1 pad_dynamic-slice_fusion.7
  24.2 0.7 broadcast_in_dim.2
  24.9 0.9 copy.37
  25.8 0.1 broadcast_compare_fusion.3
  25.9 0.2 copy.26
  26.1 0.2 copy.25
  26.3 0.1 add_bitcast_fusion
  26.3 0.2 copy.28
  26.5 0.2 copy.27
  26.7 0.1 add_bitcast_fusion.1
  26.7 0.1 rev.3
  26.8 1.2 slice_bitcast_fusion
  28.0 0.3 stack.157
  28.3 0.1 maximum_bitcast_fusion
  28.4 1.0 pad_maximum_fusion.tab_in
  29.4 0.1 add_convert_fusion.hots
  29.5 0.0 copy-start
  29.5 1.2 %copy-done = bf16[256,2048]{1,0:T(8,128)(2,1)S(1)} copy-done((bf16[256,2048]{1,0:T(8,128)(2,1)S(1)}, bf16[256,2048]{1,0:T(8,128)(2,1)}, u32[]{:S(2)}) %copy-start) | copy-done | bytes 1048600
  30.8 87.1 %shard_map.64 = bf16[256,2048]{1,0:T(8,128)(2,1)S(1)} custom-call(bf16[2,768,64]{2,1,0:T(8,128)(2,1)S(1)} %add_convert_fusion.hots, f32[6,8,2048]{2,1,0:T(8,128)S(1)} %pad_maximum_fusion.tab_in, f32[2,128,256]{2,1,0:T(8,128)S(1)} %pad_maximum_fusion.1.base_in, bf16[256,2048]{1,0:T(8,128)(2,1)S(1)} %copy-done), custom_call_target="tpu_custom_call" | custom-call | tf_op jit(solution)/shard_map/pallas_call | solution.py:322
  117.8 1.0 copy.39
  (41 shorter events, 0.3 us)
Async XLA Ops:
  29.5 1.2 %copy-start = (bf16[256,2048]{1,0:T(8,128)(2,1)S(1)}, bf16[256,2048]{1,0:T(8,128)(2,1)}, u32[]{:S(2)}) copy-start(bf16[256,2048]{1,0:T(8,128)(2,1)} %weight.1) | copy-start | bytes 3145732

commit v3 on v2

--- a/solution.py
+++ b/solution.py
@@ -273,7 +273,7 @@
 
 def one_hot(codes, offset, count, step, short_taps):
     picked = jnp.stack(
-        [lax.dynamic_slice_in_dim(codes, offset + step * k, count) for k in range(short_taps)], axis=1
+        [codes[offset + step * k : offset + step * k + count] for k in range(short_taps)], axis=1
     )
     hot = picked[:, :, None] == jnp.arange(8, dtype=jnp.int32) % 4
     hot = jnp.pad(hot, ((0, 0), (0, 1), (0, 0)))
@@ -303,14 +303,17 @@
     length = tokens.shape[0]
     window = length + taps
     me = lax.axis_index("seq")
-    codes = lax.all_gather(tokens, "seq", axis=0, tiled=True)
-    flipped = jnp.pad(3 - codes, (length, length), constant_values=-1)
-    codes = jnp.pad(codes, (length, length), constant_values=-1)
+    before = lax.ppermute(tokens, "seq", [(i, i + 1) for i in range(seq_size - 1)])
+    after = lax.ppermute(tokens, "seq", [(i + 1, i) for i in range(seq_size - 1)])
+    before = jnp.where(me == 0, -1, before)
+    after = jnp.where(me == seq_size - 1, -1, after)
+    mine = jnp.concatenate([before, tokens, after])
+    theirs = lax.ppermute(mine, "seq", [(i, i ^ 2) for i in range(seq_size)])
     hots = [[], []]
-    for index in (me, me ^ 2):
-        start = (index + 1) * length
-        hots[0].append(one_hot(codes, start - taps, window, -1, short_taps))
-        hots[1].append(one_hot(flipped, start, window, 1, short_taps))
+    for codes in (mine, theirs):
+        flipped = jnp.where(codes < 0, -1, 3 - codes)
+        hots[0].append(one_hot(codes, length - taps, window, -1, short_taps))
+        hots[1].append(one_hot(flipped, length, window, 1, short_taps))
     hots = jnp.stack([jnp.concatenate(h, axis=0) for h in hots])
     tab = tables(feature_table, short_filter, med_bias)
     base = tap_rows(med_filter)

time: 119 us -> 107 us (0.90)
  blocking collectives: 23.2 us -> 0 us
  starting transfers between devices: 0 us -> 7.69 us
  other arithmetic: 1.47 us -> 2.86 us
    all_gather x1 -> x0, blocking collectives: 23.2 us -> none  [per_device(): codes = lax.all_gather(tokens, 'seq', axis=0, tiled=True)]
    ppermute x0 -> x3, starting transfers between devices: none -> 7.69 us  [the longest x1 4.53 us: per_device(): lax.ppermute(tokens, 'seq', [(i, i + 1) for i in range(seq_size - 1)])]
  transfers between devices with their start and end apart: 0 -> 3, of which waited for: 0 -> 1; matrix products, arithmetic and copies ran while one was open for 0% -> 5% of each run, Pallas kernels for 0% -> 0%
where the time goes in v3:
time: 107 us
  Pallas kernels  88.2 us (82%)
  starting transfers between devices  7.69 us (7%)
  local copies, waits for them, and re-layouts  6.57 us (6%)
  other arithmetic  2.86 us (3%)
    pallas_call x1, Pallas kernels, per_device(): pl.pallas_call(functools.partial(kernel, sizes, taps, group_width), out_s...  88.2 us
    ppermute x1, starting transfers between devices, per_device(): lax.ppermute(tokens, 'seq', [(i, i + 1) for i in range(seq_size - 1)])  4.53 us
    unnamed x4, local copies, waits for them, and re-layouts  3.05 us
  transfers between devices with their start and end apart: 3, of which 1 were waited for; matrix products, arithmetic and copies ran while one was open for 5% of the time, Pallas kernels for 0%

profile of v3, /device:TPU:1, one launch (start us, length us, event | category | flops | bytes accessed | tf_op | source)
XLA Modules:
  0.0 106.7 jit_solution(17321214912371740410)
XLA Ops:
  0.0 4.5 %collective-permute-start = (s32[256]{0:T(256)}, s32[256]{0:T(256)S(1)}, u32[]{:S(2)}, u32[]{:S(2)}) collective-permute-start(s32[256]{0:T(256)} %param.6), channel_id=1, source_target_pairs={{0,2},{2,4},{4,6},{6,8},{8,10},{10,12},{12,14},{14,16},{16,18},{18... | collective-permute-start | bytes 3080 | tf_op jit(solution)/shard_map/ppermute | solution.py:306
  4.5 1.9 %collective-permute-start.1 = (s32[256]{0:T(256)}, s32[256]{0:T(256)S(1)}, u32[]{:S(2)}, u32[]{:S(2)}) collective-permute-start(s32[256]{0:T(256)} %param.6), channel_id=1, source_target_pairs={{2,0},{4,2},{6,4},{8,6},{10,8},{12,10},{14,12},{16,14},{18,16},{20... | collective-permute-start | bytes 3080 | tf_op jit(solution)/shard_map/ppermute | solution.py:307
  6.5 0.1 pad.22.clone
  6.6 0.9 copy.24
  7.4 0.1 rev.3
  7.5 1.2 %slice_bitcast_fusion = (bf16[3,1,2048]{2,1,0:T(2,128)(2,1)S(1)}, bf16[3,1,2048]{2,1,0:T(2,128)(2,1)S(1)}, bf16[3,1,2048]{2,1,0:T(2,128)(2,1)S(1)}, bf16[3,1,2048]{2,1,0:T(2,128)(2,1)S(1)}) fusion(bf16[512,3,2048]{2,0,1:T(8,128)(2,1)} %param.7), kind=kLoop, calls=%fused_computation.16 | loop fusion | bytes 98304 | tf_op jit(solution)/shard_map/stack;squeeze | solution.py:292
  8.7 0.3 stack.157
  9.0 0.1 maximum_bitcast_fusion
  9.1 0.7 broadcast_in_dim.24
  9.8 1.0 pad_maximum_fusion.tab_in
  10.9 0.0 collective-permute-done
  10.9 0.7 pad_add_fusion.1
  11.6 0.0 collective-permute-done.1
  11.6 0.7 subtract_select_fusion.1
  12.3 0.1 fusion.1
  12.3 1.2 %collective-permute-start.2 = (s32[768]{0:T(1024)S(1)}, s32[768]{0:T(1024)S(1)}, u32[]{:S(2)}, u32[]{:S(2)}) collective-permute-start(s32[768]{0:T(1024)S(1)} %get-tuple-element.31), channel_id=1, source_target_pairs={{0,4},{2,6},{4,0},{6,2},{8,12},{10,14},{12,8},{14,10},{16,20},{18,... | collective-permute-start | bytes 9224 | tf_op jit(solution)/shard_map/ppermute | solution.py:311
  13.6 0.1 fusion.3
  13.9 0.9 collective-permute-done.2
  14.8 0.1 fusion
  15.0 0.1 fusion.2
  15.1 0.1 broadcast_compare_fusion.3
  15.3 0.2 copy.13
  15.5 0.2 copy.12
  15.7 0.2 copy.15
  15.8 0.2 copy.14
  16.0 0.1 add_bitcast_fusion
  16.1 0.1 add_bitcast_fusion.1
  16.1 0.1 add_convert_fusion.hots
  16.2 0.0 copy-start
  16.3 1.2 %copy-done = bf16[256,2048]{1,0:T(8,128)(2,1)S(1)} copy-done((bf16[256,2048]{1,0:T(8,128)(2,1)S(1)}, bf16[256,2048]{1,0:T(8,128)(2,1)}, u32[]{:S(2)}) %copy-start) | copy-done | bytes 1048600
  17.5 88.2 %shard_map.64 = bf16[256,2048]{1,0:T(8,128)(2,1)S(1)} custom-call(bf16[2,768,64]{2,1,0:T(8,128)(2,1)S(1)} %add_convert_fusion.hots, f32[6,8,2048]{2,1,0:T(8,128)S(1)} %pad_maximum_fusion.tab_in, f32[2,128,256]{2,1,0:T(8,128)S(1)} %pad_maximum_fusion.1.base_in, bf16[256,2048]{1,0:T(8,128)(2,1)S(1)} %copy-done), custom_call_target="tpu_custom_call" | custom-call | tf_op jit(solution)/shard_map/pallas_call | solution.py:325
  105.7 1.0 copy.26
  (43 shorter events, 0.3 us)
Async XLA Ops:
  0.0 10.9 %collective-permute-start = (s32[256]{0:T(256)}, s32[256]{0:T(256)S(1)}, u32[]{:S(2)}, u32[]{:S(2)}) collective-permute-start(s32[256]{0:T(256)} %param.6), channel_id=1, source_target_pairs={{0,2},{2,4},{4,6},{6,8},{8,10},{10,12},{12,14},{14,16},{16,18},{18... | collective-permute-start | bytes 3080 | tf_op jit(solution)/shard_map/ppermute | solution.py:306
  4.5 7.0 %collective-permute-start.1 = (s32[256]{0:T(256)}, s32[256]{0:T(256)S(1)}, u32[]{:S(2)}, u32[]{:S(2)}) collective-permute-start(s32[256]{0:T(256)} %param.6), channel_id=1, source_target_pairs={{2,0},{4,2},{6,4},{8,6},{10,8},{12,10},{14,12},{16,14},{18,16},{20... | collective-permute-start | bytes 3080 | tf_op jit(solution)/shard_map/ppermute | solution.py:307
  12.3 2.5 %collective-permute-start.2 = (s32[768]{0:T(1024)S(1)}, s32[768]{0:T(1024)S(1)}, u32[]{:S(2)}, u32[]{:S(2)}) collective-permute-start(s32[768]{0:T(1024)S(1)} %get-tuple-element.31), channel_id=1, source_target_pairs={{0,4},{2,6},{4,0},{6,2},{8,12},{10,14},{12,8},{14,10},{16,20},{18,... | collective-permute-start | bytes 9224 | tf_op jit(solution)/shard_map/ppermute | solution.py:311
  16.2 1.2 %copy-start = (bf16[256,2048]{1,0:T(8,128)(2,1)S(1)}, bf16[256,2048]{1,0:T(8,128)(2,1)}, u32[]{:S(2)}) copy-start(bf16[256,2048]{1,0:T(8,128)(2,1)} %weight.1) | copy-start | bytes 3145732

commit v4 on v3

--- a/solution.py
+++ b/solution.py
@@ -81,7 +81,9 @@
     rows, width = weight.shape
     half = width // 2
     length = out.shape[0]
-    tile = min(256, half)
+    parts, _, _, part_width = pieces.shape
+    tile = min(256, part_width)
+    part_tiles = part_width // tile
     tiles = half // tile
 
     def place(o, yy, cc):
@@ -114,42 +116,55 @@
             device_id=other, device_id_type=MESH,
         )
 
-    def piece(o, yy, cc):
+    def piece(part, o, yy, cc):
         start = pl.multiple_of((yy * 2 + cc) * rows, rows)
-        return pieces.at[o, pl.ds(start, rows)]
-
-    def columns_of(which):
-        return weight.at[:, pl.ds(pl.multiple_of(which * half, half), half)]
+        return pieces.at[part, o, pl.ds(start, rows)]
+
+    def columns_of(part, which):
+        start = pl.multiple_of(which * half + part * part_width, part_width)
+        return weight.at[:, pl.ds(start, part_width)]
 
     def sub_y(sub):
         return y if sub == 0 else 1 - y
 
-    def forwards(origin, sub, action, own=False):
+    def forwards(part, origin, sub, action, own=False):
         yy = sub_y(sub)
-        dst = piece(origin, yy, core)
-        src = columns_of(y) if own else dst
-        receive = recv.at[origin, yy * 2 + core]
+        dst = piece(part, origin, yy, core)
+        src = columns_of(part, y) if own else dst
+        receive = recv.at[part, origin, yy * 2 + core]
 
         @pl.when((origin <= outer) & (outer < outer_size - 1))
         def _():
-            action(remote(src, dst, up_send.at[origin, sub], receive, {"seq": me + 4}))
+            action(remote(src, dst, up_send.at[part, origin, sub], receive, {"seq": me + 4}))
 
         @pl.when((origin >= outer) & (outer > 0))
         def _():
-            action(remote(src, dst, down_send.at[origin, sub], receive, {"seq": me - 4}))
-
-        action(remote(src, dst, side_send.at[origin, sub], receive, {"seq": side}))
-
-    def arrived(origin, slot):
+            action(remote(src, dst, down_send.at[part, origin, sub], receive, {"seq": me - 4}))
+
+        action(remote(src, dst, side_send.at[part, origin, sub], receive, {"seq": side}))
+
+    def arrived(part, origin, slot):
         start = pl.multiple_of(slot * rows, rows)
-        dst = pieces.at[origin, pl.ds(start, rows)]
-        remote(dst, dst, y_send, recv.at[origin, slot], {"seq": across}).wait_recv()
-
-    y_copy = remote(
-        columns_of(1 - y), piece(outer, y, core), y_send, recv.at[outer, y * 2 + core], {"seq": across}
-    )
-    y_copy.start()
-    forwards(outer, 0, lambda c: c.start(), own=True)
+        dst = pieces.at[part, origin, pl.ds(start, rows)]
+        remote(dst, dst, y_send.at[part], recv.at[part, origin, slot], {"seq": across}).wait_recv()
+
+    def start(copy):
+        copy.start()
+
+    def wait_send(copy):
+        copy.wait_send()
+
+    y_copies = [
+        remote(
+            columns_of(part, 1 - y), piece(part, outer, y, core), y_send.at[part],
+            recv.at[part, outer, y * 2 + core], {"seq": across},
+        )
+        for part in range(parts)
+    ]
+    y_copies[0].start()
+    forwards(0, outer, 0, start, own=True)
+    for copy in y_copies[1:]:
+        copy.start()
     tab_copies = []
     for step in range(1, ch_size):
         other = {"ch": lax.rem(ch + step, ch_size)}
@@ -158,9 +173,13 @@
             copy.start()
             tab_copies.append(copy)
     local_copies = [
-        pltpu.make_async_copy(columns_of(y), piece(outer, y, core), local_sem.at[0]),
-        pltpu.make_async_copy(tab_in, tabs.at[ch], local_sem.at[1]),
-        pltpu.make_async_copy(base_in, bases.at[ch], local_sem.at[2]),
+        pltpu.make_async_copy(tab_in, tabs.at[ch], local_sem.at[0]),
+        pltpu.make_async_copy(base_in, bases.at[ch], local_sem.at[1]),
+    ] + [
+        pltpu.make_async_copy(
+            columns_of(part, y), piece(part, outer, y, core), local_sem.at[2 + part]
+        )
+        for part in range(parts)
     ]
     for copy in local_copies:
         copy.start()
@@ -191,84 +210,113 @@
         mixed[:, pl.ds(pl.multiple_of((owner * per_ch + inner) * LANES, LANES), LANES)] = value
         return carry
 
-    def event(t, sub):
+    def event(part, t, sub):
         yy = sub_y(sub)
         if t == 0:
-            arrived(outer, yy * 2 + core)
-            forwards(outer, sub, lambda c: c.start())
+            if sub == 1:
+                arrived(part, outer, yy * 2 + core)
+            forwards(part, outer, sub, start, own=sub == 0)
             return
 
         @pl.when(outer >= t)
         def _():
-            arrived(outer - t, yy * 2 + core)
-            forwards(outer - t, sub, lambda c: c.start())
+            arrived(part, outer - t, yy * 2 + core)
+            forwards(part, outer - t, sub, start)
 
         @pl.when(outer + t < outer_size)
         def _():
-            arrived(outer + t, yy * 2 + core)
-            forwards(outer + t, sub, lambda c: c.start())
-
-    events = [(t, sub) for t in range(outer_size) for sub in range(2)][1:]
-    done = 0
-    for number, (t, sub) in enumerate(events):
-        upto = steps * (number + 1) // len(events)
-        if upto > done:
-            lax.fori_loop(done, upto, block, 0)
-        done = upto
-        event(t, sub)
-
-    def side_wait(o, carry):
-        for yy in range(2):
-            arrived(o, yy * 2 + 1 - core)
+            arrived(part, outer + t, yy * 2 + core)
+            forwards(part, outer + t, sub, start)
+
+    both = (0, 1)
+    events = [(0, t, sub) for t in range(outer_size - 1) for sub in both][1:]
+    for part in range(1, parts):
+        events += [(part, 0, sub) for sub in both]
+        events += [(part - 1, outer_size - 1, sub) for sub in both]
+        events += [(part, t, sub) for t in range(1, outer_size - 1) for sub in both]
+    last = [(parts - 1, outer_size - 1, sub) for sub in both]
+    due = {}
+    for number, item in enumerate(events):
+        due.setdefault(max(0, steps * (number + 1) // len(events) - 1), []).append(item)
+
+    def step(i, carry):
+        block(i, carry)
+        for when, items in due.items():
+
+            @pl.when(i == when)
+            def _():
+                for item in items:
+                    event(*item)
+
         return carry
 
-    lax.fori_loop(0, outer_size, side_wait, 0)
-
+    lax.fori_loop(0, steps, step, 0)
     depth = 4 * rows
 
+    def side_waits(part):
+        def wait(o, carry):
+            for yy in both:
+                arrived(part, o, yy * 2 + 1 - core)
+            return carry
+
+        lax.fori_loop(0, outer_size, wait, 0)
+
     def product(position, n):
+        part, inside = n // part_tiles, n % part_tiles
         total = None
         for o in range(outer_size):
-            part = dot(
+            term = dot(
                 mixed[position : position + length, o * depth : (o + 1) * depth],
-                pieces[o, :, n * tile : (n + 1) * tile],
+                pieces[part, o, :, inside * tile : (inside + 1) * tile],
             )
-            total = part if total is None else total + part
+            total = term if total is None else total + term
         return total.astype(jnp.bfloat16)
 
-    def out_columns(n):
-        return out.at[:, pl.ds(pl.multiple_of(y * half + n * tile, tile), tile)]
+    def out_columns(which, n):
+        return pl.ds(pl.multiple_of(which * half + n * tile, tile), tile)
 
     out_copies = []
+    for part in range(parts):
+        numbers = range(part * part_tiles, (part + 1) * part_tiles)
+        final = part == parts - 1
+        if final:
+            for item in last[1:]:
+                event(*item)
+        side_waits(part)
+        for n in numbers:
+            stage[n] = product(length, n)
+            copy = remote(
+                stage.at[n], out.at[:, out_columns(y, n)], out_send.at[n], out_recv.at[n], {"seq": across}
+            )
+            copy.start()
+            out_copies.append(copy)
+        if part == parts - 2:
+            event(*last[0])
+        for n in numbers:
+            out[:, out_columns(y, n)] = product(0, n)
+
+    for copy in y_copies + tab_copies:
+        copy.wait_send()
+    for part in range(parts):
+        for t in range(outer_size):
+            for sub in both:
+                if t == 0:
+                    forwards(part, outer, sub, wait_send, own=sub == 0)
+                    continue
+
+                @pl.when(outer >= t)
+                def _():
+                    forwards(part, outer - t, sub, wait_send)
+
+                @pl.when(outer + t < outer_size)
+                def _():
+                    forwards(part, outer + t, sub, wait_send)
+
     for n in range(tiles):
-        stage[n] = product(length, n)
-        copy = remote(stage.at[n], out_columns(n), out_send.at[n], out_recv.at[n], {"seq": across})
-        copy.start()
-        out_copies.append(copy)
-    for n in range(tiles):
-        out[:, pl.ds(pl.multiple_of(y * half + n * tile, tile), tile)] = product(0, n)
-
-    y_copy.wait_send()
-    for copy in tab_copies:
-        copy.wait_send()
-    for t in range(outer_size):
-        for sub in range(2):
-            if t == 0:
-                forwards(outer, sub, lambda c: c.wait_send(), own=sub == 0)
-                continue
-
-            @pl.when(outer >= t)
-            def _():
-                forwards(outer - t, sub, lambda c: c.wait_send())
-
-            @pl.when(outer + t < outer_size)
-            def _():
-                forwards(outer + t, sub, lambda c: c.wait_send())
-
-    for n in range(tiles):
-        theirs = out.at[:, pl.ds(pl.multiple_of((1 - y) * half + n * tile, tile), tile)]
         out_copies[n].wait_send()
-        remote(stage.at[n], theirs, out_send.at[n], out_recv.at[n], {"seq": across}).wait_recv()
+        remote(
+            stage.at[n], out.at[:, out_columns(1 - y, n)], out_send.at[n], out_recv.at[n], {"seq": across}
+        ).wait_recv()
 
 
 def one_hot(codes, offset, count, step, short_taps):
@@ -319,7 +367,8 @@
     base = tap_rows(med_filter)
     outer_size = seq_size // 4
     half = width // 2
-    tile = min(256, half)
+    parts = 2
+    tile = min(256, half // parts)
     tiles = half // tile
     dma = pltpu.SemaphoreType.DMA
     return pl.pallas_call(
@@ -330,17 +379,17 @@
         scratch_shapes=[
             pltpu.VMEM((ch_size,) + tab.shape, jnp.float32),
             pltpu.VMEM((ch_size,) + base.shape, jnp.float32),
-            pltpu.VMEM((outer_size, 4 * rows, half), jnp.bfloat16),
+            pltpu.VMEM((parts, outer_size, 4 * rows, half // parts), jnp.bfloat16),
             pltpu.VMEM((2 * length, ch_size * width), jnp.bfloat16),
             pltpu.VMEM((tiles, length, tile), jnp.bfloat16),
             dma((2, ch_size)),
             dma((2, ch_size)),
-            dma((3,)),
-            dma,
-            dma((outer_size, 2)),
-            dma((outer_size, 2)),
-            dma((outer_size, 2)),
-            dma((outer_size, 4)),
+            dma((2 + parts,)),
+            dma((parts,)),
+            dma((parts, outer_size, 2)),
+            dma((parts, outer_size, 2)),
+            dma((parts, outer_size, 2)),
+            dma((parts, outer_size, 4)),
             dma((tiles,)),
             dma((tiles,)),
         ],

time: 107 us -> 102 us (0.953)
  Pallas kernels: 88.2 us -> 82.9 us
    pallas_call x1, Pallas kernels: 88.2 us -> 82.9 us  [per_device(): pl.pallas_call(functools.partial(kernel, sizes, taps, group_width), out_s...]
where the time goes in v4:
time: 102 us; the launch traced here: 101 us
  Pallas kernels  82.9 us (81%)
  starting transfers between devices  7.69 us (8%)
  local copies, waits for them, and re-layouts  6.57 us (6%)
  other arithmetic  2.86 us (3%)
    pallas_call x1, Pallas kernels, per_device(): pl.pallas_call(functools.partial(kernel, sizes, taps, group_width), out_s...  82.9 us
    ppermute x1, starting transfers between devices, per_device(): lax.ppermute(tokens, 'seq', [(i, i + 1) for i in range(seq_size - 1)])  4.53 us
    unnamed x4, local copies, waits for them, and re-layouts  3.05 us
  transfers between devices with their start and end apart: 3, of which 1 were waited for; matrix products, arithmetic and copies ran while one was open for 5% of the time, Pallas kernels for 0%

profile of v4, /device:TPU:1, one launch (start us, length us, event | category | flops | bytes accessed | tf_op | source)
XLA Modules:
  0.0 101.4 jit_solution(2129518956639025801)
XLA Ops:
  0.0 4.5 %collective-permute-start = (s32[256]{0:T(256)}, s32[256]{0:T(256)S(1)}, u32[]{:S(2)}, u32[]{:S(2)}) collective-permute-start(s32[256]{0:T(256)} %param.6), channel_id=1, source_target_pairs={{0,2},{2,4},{4,6},{6,8},{8,10},{10,12},{12,14},{14,16},{16,18},{18... | collective-permute-start | bytes 3080 | tf_op jit(solution)/shard_map/ppermute | solution.py:354
  4.5 1.9 %collective-permute-start.1 = (s32[256]{0:T(256)}, s32[256]{0:T(256)S(1)}, u32[]{:S(2)}, u32[]{:S(2)}) collective-permute-start(s32[256]{0:T(256)} %param.6), channel_id=1, source_target_pairs={{2,0},{4,2},{6,4},{8,6},{10,8},{12,10},{14,12},{16,14},{18,16},{20... | collective-permute-start | bytes 3080 | tf_op jit(solution)/shard_map/ppermute | solution.py:355
  6.5 0.1 pad.22.clone
  6.6 0.9 copy.24
  7.4 0.1 rev.3
  7.5 1.2 %slice_bitcast_fusion = (bf16[3,1,2048]{2,1,0:T(2,128)(2,1)S(1)}, bf16[3,1,2048]{2,1,0:T(2,128)(2,1)S(1)}, bf16[3,1,2048]{2,1,0:T(2,128)(2,1)S(1)}, bf16[3,1,2048]{2,1,0:T(2,128)(2,1)S(1)}) fusion(bf16[512,3,2048]{2,0,1:T(8,128)(2,1)} %param.7), kind=kLoop, calls=%fused_computation.16 | loop fusion | bytes 98304 | tf_op jit(solution)/shard_map/stack;squeeze | solution.py:340
  8.7 0.3 stack.157
  9.0 0.1 maximum_bitcast_fusion
  9.1 0.7 broadcast_in_dim.24
  9.8 1.0 pad_maximum_fusion.tab_in
  10.9 0.0 collective-permute-done
  10.9 0.7 pad_add_fusion.1
  11.6 0.0 collective-permute-done.1
  11.6 0.7 subtract_select_fusion.1
  12.3 0.1 fusion.1
  12.3 1.2 %collective-permute-start.2 = (s32[768]{0:T(1024)S(1)}, s32[768]{0:T(1024)S(1)}, u32[]{:S(2)}, u32[]{:S(2)}) collective-permute-start(s32[768]{0:T(1024)S(1)} %get-tuple-element.31), channel_id=1, source_target_pairs={{0,4},{2,6},{4,0},{6,2},{8,12},{10,14},{12,8},{14,10},{16,20},{18,... | collective-permute-start | bytes 9224 | tf_op jit(solution)/shard_map/ppermute | solution.py:359
  13.6 0.1 fusion.3
  13.9 0.9 collective-permute-done.2
  14.8 0.1 fusion
  15.0 0.1 fusion.2
  15.1 0.1 broadcast_compare_fusion.3
  15.3 0.2 copy.13
  15.5 0.2 copy.12
  15.7 0.2 copy.15
  15.8 0.2 copy.14
  16.0 0.1 add_bitcast_fusion
  16.1 0.1 add_bitcast_fusion.1
  16.1 0.1 add_convert_fusion.hots
  16.2 0.0 copy-start
  16.3 1.2 %copy-done = bf16[256,2048]{1,0:T(8,128)(2,1)S(1)} copy-done((bf16[256,2048]{1,0:T(8,128)(2,1)S(1)}, bf16[256,2048]{1,0:T(8,128)(2,1)}, u32[]{:S(2)}) %copy-start) | copy-done | bytes 1048600
  17.5 82.9 %shard_map.64 = bf16[256,2048]{1,0:T(8,128)(2,1)S(1)} custom-call(bf16[2,768,64]{2,1,0:T(8,128)(2,1)S(1)} %add_convert_fusion.hots, f32[6,8,2048]{2,1,0:T(8,128)S(1)} %pad_maximum_fusion.tab_in, f32[2,128,256]{2,1,0:T(8,128)S(1)} %pad_maximum_fusion.1.base_in, bf16[256,2048]{1,0:T(8,128)(2,1)S(1)} %copy-done), custom_call_target="tpu_custom_call" | custom-call | tf_op jit(solution)/shard_map/pallas_call | solution.py:374
  100.4 1.0 copy.26
  (43 shorter events, 0.3 us)
Async XLA Ops:
  0.0 10.9 %collective-permute-start = (s32[256]{0:T(256)}, s32[256]{0:T(256)S(1)}, u32[]{:S(2)}, u32[]{:S(2)}) collective-permute-start(s32[256]{0:T(256)} %param.6), channel_id=1, source_target_pairs={{0,2},{2,4},{4,6},{6,8},{8,10},{10,12},{12,14},{14,16},{16,18},{18... | collective-permute-start | bytes 3080 | tf_op jit(solution)/shard_map/ppermute | solution.py:354
  4.5 7.0 %collective-permute-start.1 = (s32[256]{0:T(256)}, s32[256]{0:T(256)S(1)}, u32[]{:S(2)}, u32[]{:S(2)}) collective-permute-start(s32[256]{0:T(256)} %param.6), channel_id=1, source_target_pairs={{2,0},{4,2},{6,4},{8,6},{10,8},{12,10},{14,12},{16,14},{18,16},{20... | collective-permute-start | bytes 3080 | tf_op jit(solution)/shard_map/ppermute | solution.py:355
  12.3 2.5 %collective-permute-start.2 = (s32[768]{0:T(1024)S(1)}, s32[768]{0:T(1024)S(1)}, u32[]{:S(2)}, u32[]{:S(2)}) collective-permute-start(s32[768]{0:T(1024)S(1)} %get-tuple-element.31), channel_id=1, source_target_pairs={{0,4},{2,6},{4,0},{6,2},{8,12},{10,14},{12,8},{14,10},{16,20},{18,... | collective-permute-start | bytes 9224 | tf_op jit(solution)/shard_map/ppermute | solution.py:359
  16.2 1.2 %copy-start = (bf16[256,2048]{1,0:T(8,128)(2,1)S(1)}, bf16[256,2048]{1,0:T(8,128)(2,1)}, u32[]{:S(2)}) copy-start(bf16[256,2048]{1,0:T(8,128)(2,1)} %weight.1) | copy-start | bytes 3145732
